TPU v7x, 512 devices: a whole 4x8x8 slice. The times are simulated.
512 devices in a mesh: dp: 32 (over z, y_lo), ctx: 16 (over x, y_hi, core).
Axes of the slice: x: 4, y: 8 (y_hi: 2, y_lo: 4; y = y_hi * 4 + y_lo), z: 8, core: 2. Of those that a mesh axis runs over, the one named last changes fastest.
Arguments:
- frame_input: bfloat16 [64, 1024, 1536], P('dp', 'ctx'), may hold values from -6 to 6
- queries: bfloat16 [64, 1024, 768], P('dp', 'ctx'), may hold values from -18 to 18
- key_proj: bfloat16 [64, 1024, 768], P('dp', 'ctx'), may hold values from -18 to 18
- value_proj: bfloat16 [64, 1024, 768], P('dp', 'ctx'), may hold values from -6 to 6
- out_weight: bfloat16 [1536, 768], P('ctx', 'dp'), may hold values from -0.21875 to 0.21875
- conv_weight: bfloat16 [31, 1536], P(None, 'dp'), may hold values from -1 to 1
- lengths: int32 [64], P('dp'), may hold values from 256 to 1024, as said below
- grad_output: bfloat16 [64, 1024, 1536], P('dp', 'ctx'), may hold values from -6 to 6
Outputs:
- block_output: bfloat16 [64, 1024, 1536], P('dp', 'ctx')
- grad_input: bfloat16 [64, 1024, 1536], P('dp', 'ctx')
- grad_queries: bfloat16 [64, 1024, 768], P('dp', 'ctx')
- grad_keys: bfloat16 [64, 1024, 768], P('dp', 'ctx')
- grad_values: bfloat16 [64, 1024, 768], P('dp', 'ctx')
- grad_out_weight: float32 [1536, 768], P('ctx', 'dp')
- grad_conv_weight: float32 [31, 1536], P(None, 'dp')
Inputs may be any that keep to these rules, and one draw needn't show every extreme that they name: `lengths`: at least one utterance of every draw fills all 1024 frame slots.
All inputs are finite; a program needn't handle non-finite values.
Results may differ from a plain program's by a relative error of at most 0.035.
Values may be sent and summed in bfloat16 or wider, within the bound.
A program may use at most 128 MiB of HBM per device.

v0:
```python
import jax
import jax.numpy as jnp
from jax import lax
from jax.sharding import PartitionSpec as P

HEAD_DIM = 64
masked_score = -1e30


def padded_2(array, sides, width):
    for axis, dim in sides:
        size, length = (lax.axis_size(axis), array.shape[dim])
        up = [(i, (i + 1) % size) for i in range(size - 1)]
        down = [(j, i) for i, j in up]
        last = lax.slice_in_dim(array, length - width, length, axis=dim)
        leading = lax.slice_in_dim(array, 0, width, axis=dim)
        before = lax.ppermute(last, axis, up)
        after = lax.ppermute(leading, axis, down)
        array = jnp.concatenate([before, array, after], axis=dim)
    return array


def depthwise(lhs, rhs):
    return lax.conv_general_dilated(
        lhs,
        rhs,
        (1,),
        "VALID",
        dimension_numbers=("NWC", "WIO", "NWC"),
        feature_group_count=lhs.shape[2],
        precision=lax.Precision.HIGHEST,
    )


def per_device(
    frame_input, queries, key_proj, value_proj, out_weight, conv_weight, lengths, grad_output
):
    utt_count = frame_input.shape[0]
    frame_count = frame_input.shape[1]
    inner_width = queries.shape[2]
    head_count = inner_width // HEAD_DIM
    group_heads = max((g for g in range(1, 7) if head_count % g == 0))
    group_count = head_count // group_heads
    group_width = group_heads * HEAD_DIM
    tap_count = conv_weight.shape[0]
    half_span = (tap_count - 1) // 2
    score_scale = HEAD_DIM ** (-0.5)
    total_frames = frame_count * lax.axis_size("ctx")
    offset = lax.axis_index("ctx") * frame_count
    own_valid = (offset + jnp.arange(frame_count, dtype=jnp.int32))[None, :] < lengths[:, None]
    all_valid = jnp.arange(total_frames, dtype=jnp.int32)[None, :] < lengths[:, None]

    def grouped(values):
        row_count = values.shape[1]
        return values.reshape(utt_count, row_count, group_count, group_width).transpose(2, 0, 1, 3)

    def ungrouped(values):
        row_count = values.shape[2]
        return values.transpose(1, 2, 0, 3).reshape(utt_count, row_count, group_count * group_width)

    def split_heads(values):
        return values.reshape(utt_count, values.shape[1], group_heads, HEAD_DIM)

    def stats_grouped(values):
        row_count = values.shape[1]
        return values.reshape(utt_count, row_count, group_count, group_heads).transpose(2, 0, 3, 1)

    def masked_scores(query_block, key_block, key_mask):
        scores = (
            jnp.einsum(
                "uqgd,ukgd->ugqk", query_block, key_block, preferred_element_type=jnp.float32
            )
            * score_scale
        )
        return jnp.where(key_mask[:, None, None, :], scores, masked_score)

    taps = lax.all_gather(conv_weight, "dp", axis=1, tiled=True).astype(jnp.float32)
    panel_rows = lax.all_gather(out_weight, "dp", axis=1, tiled=True)
    weight_full = lax.all_gather(panel_rows, "ctx", axis=0, tiled=True)
    all_keys, all_values = (
        lax.all_gather(key_proj, "ctx", axis=1, tiled=True),
        lax.all_gather(value_proj, "ctx", axis=1, tiled=True),
    )
    query_groups = grouped(queries)
    key_groups = grouped(all_keys)
    value_groups = grouped(all_values)

    def forward_group(unused, items):
        query_group, key_group, value_group = items
        query_block = split_heads(query_group)
        scores = masked_scores(query_block, split_heads(key_group), all_valid)
        largest = jnp.max(scores, axis=-1)
        log_group = largest + jnp.log(jnp.sum(jnp.exp(scores - largest[..., None]), axis=-1))
        weights_low = jnp.exp(scores - log_group[..., None]).astype(jnp.bfloat16)
        attended_group = jnp.einsum(
            "ugqk,ukgd->uqgd",
            weights_low,
            split_heads(value_group),
            preferred_element_type=jnp.float32,
        )
        return (None, (log_group, attended_group.reshape(utt_count, frame_count, group_width)))

    _, (log_groups, attended_groups) = lax.scan(
        forward_group, None, (query_groups, key_groups, value_groups)
    )
    attended = ungrouped(attended_groups).astype(jnp.bfloat16)
    log_total = log_groups.transpose(1, 3, 0, 2).reshape(utt_count, frame_count, head_count)
    projected = jnp.einsum("ufe,de->ufd", attended, weight_full, preferred_element_type=jnp.float32)
    hidden = (frame_input.astype(jnp.float32) + projected).astype(jnp.bfloat16)
    masked_hidden = jnp.where(own_valid[:, :, None], hidden, jnp.zeros_like(hidden))
    padded = padded_2(masked_hidden, (("ctx", 1),), half_span).astype(jnp.float32)
    conv_sum = depthwise(padded, taps[:, None, :])
    sigmoid = jax.nn.sigmoid(conv_sum)
    block_output = (hidden.astype(jnp.float32) + conv_sum * sigmoid).astype(jnp.bfloat16)
    grad_local = grad_output.astype(jnp.float32)
    swish_slope = sigmoid * (1.0 + conv_sum * (1.0 - sigmoid))
    grad_conv = (grad_local * swish_slope).astype(jnp.bfloat16)
    grad_padded = padded_2(grad_conv, (("ctx", 1),), half_span).astype(jnp.float32)
    back_sum = depthwise(grad_padded, taps[::-1][:, None, :])
    grad_hidden = (grad_local + jnp.where(own_valid[:, :, None], back_sum, 0.0)).astype(
        jnp.bfloat16
    )
    grad_conv_wide = grad_conv.astype(jnp.float32)
    kernel_term = jnp.zeros((tap_count, conv_sum.shape[2]), jnp.float32)
    for utt_index in range(utt_count):
        kernel_term = (
            kernel_term
            + depthwise(padded[utt_index : utt_index + 1], grad_conv_wide[utt_index][:, None, :])[0]
        )
    kernel_whole = lax.psum(kernel_term.astype(jnp.bfloat16), "ctx")
    grad_conv_weight = lax.psum_scatter(kernel_whole, "dp", scatter_dimension=1, tiled=True).astype(
        jnp.float32
    )
    grad_attended = jnp.einsum(
        "ufd,de->ufe", grad_hidden, weight_full, preferred_element_type=jnp.float32
    ).astype(jnp.bfloat16)
    row_delta = jnp.sum(
        grad_attended.astype(jnp.float32).reshape(utt_count, frame_count, head_count, HEAD_DIM)
        * attended.astype(jnp.float32).reshape(utt_count, frame_count, head_count, HEAD_DIM),
        axis=-1,
    )
    grad_groups = grouped(grad_attended)

    def query_group_step(unused, items):
        query_group, key_group, value_group, grad_group, log_group, delta_group = items
        key_block = split_heads(key_group)
        weights = jnp.exp(
            masked_scores(split_heads(query_group), key_block, all_valid) - log_group[..., None]
        )
        grad_weights = jnp.einsum(
            "uqgd,ukgd->ugqk",
            split_heads(grad_group),
            split_heads(value_group),
            preferred_element_type=jnp.float32,
        )
        grad_scores = (weights * (grad_weights - delta_group[..., None])).astype(jnp.bfloat16)
        query_sum = jnp.einsum(
            "ugqk,ukgd->uqgd", grad_scores, key_block, preferred_element_type=jnp.float32
        )
        return (None, query_sum.reshape(utt_count, frame_count, group_width))

    _, query_sums = lax.scan(
        query_group_step,
        None,
        (
            query_groups,
            key_groups,
            value_groups,
            grad_groups,
            stats_grouped(log_total),
            stats_grouped(row_delta),
        ),
    )
    grad_queries = (ungrouped(query_sums) * score_scale).astype(jnp.bfloat16)
    total_log, total_delta = (
        lax.all_gather(log_total, "ctx", axis=1, tiled=True),
        lax.all_gather(row_delta, "ctx", axis=1, tiled=True),
    )
    own_key_groups = grouped(key_proj)
    own_value_groups = grouped(value_proj)
    group_zeros = jnp.zeros((group_count, utt_count, frame_count, group_width), jnp.float32)
    start_sums = (group_zeros, group_zeros)
    query_all, grad_all = (
        lax.all_gather(queries, "ctx", axis=1, tiled=True),
        lax.all_gather(grad_attended, "ctx", axis=1, tiled=True),
    )
    log_piece = stats_grouped(total_log)
    delta_piece = stats_grouped(total_delta)

    def key_group_step(unused, items):
        (
            query_group,
            grad_group,
            log_group,
            delta_group,
            key_group,
            value_group,
            key_sum,
            value_sum,
        ) = items
        query_block = split_heads(query_group)
        grad_block = split_heads(grad_group)
        weights = jnp.exp(
            masked_scores(query_block, split_heads(key_group), own_valid) - log_group[..., None]
        )
        grad_weights = jnp.einsum(
            "uqgd,ukgd->ugqk",
            grad_block,
            split_heads(value_group),
            preferred_element_type=jnp.float32,
        )
        grad_scores = (weights * (grad_weights - delta_group[..., None])).astype(jnp.bfloat16)
        key_next = key_sum + jnp.einsum(
            "ugqk,uqgd->ukgd", grad_scores, query_block, preferred_element_type=jnp.float32
        ).reshape(utt_count, frame_count, group_width)
        value_next = value_sum + jnp.einsum(
            "ugqk,uqgd->ukgd",
            weights.astype(jnp.bfloat16),
            grad_block,
            preferred_element_type=jnp.float32,
        ).reshape(utt_count, frame_count, group_width)
        return (None, (key_next, value_next))

    _, result_sums = lax.scan(
        key_group_step,
        None,
        (
            grouped(query_all),
            grouped(grad_all),
            log_piece,
            delta_piece,
            own_key_groups,
            own_value_groups,
            start_sums[0],
            start_sums[1],
        ),
    )
    key_sum, value_sum = result_sums
    grad_keys = (ungrouped(key_sum) * score_scale).astype(jnp.bfloat16)
    grad_values = ungrouped(value_sum).astype(jnp.bfloat16)
    hidden_cols = lax.slice_in_dim(
        grad_hidden, 0, weight_full.shape[0] // lax.axis_size("ctx") * lax.axis_size("ctx"), axis=2
    )
    panel_share = lax.psum_scatter(
        jnp.einsum("ufd,ufe->de", hidden_cols, attended, preferred_element_type=jnp.float32).astype(
            jnp.bfloat16
        ),
        "ctx",
        scatter_dimension=0,
        tiled=True,
    )
    grad_out_weight = lax.psum_scatter(panel_share, "dp", scatter_dimension=1, tiled=True).astype(
        jnp.float32
    )
    return (
        block_output,
        grad_hidden,
        grad_queries,
        grad_keys,
        grad_values,
        grad_out_weight,
        grad_conv_weight,
    )


def solution(mesh):
    placed = (
        P("dp", "ctx", None),
        P("dp", "ctx", None),
        P("dp", "ctx", None),
        P("dp", "ctx", None),
        P("ctx", "dp"),
        P(None, "dp"),
        P("dp"),
        P("dp", "ctx", None),
    )
    return jax.shard_map(
        per_device,
        mesh=mesh,
        in_specs=placed,
        out_specs=(
            P("dp", "ctx", None),
            P("dp", "ctx", None),
            P("dp", "ctx", None),
            P("dp", "ctx", None),
            P("dp", "ctx", None),
            P("ctx", "dp"),
            P(None, "dp"),
        ),
        check_vma=False,
    )
```

profile of v0, /device:TPU:1, one launch (start us, length us, event | category | flops | bytes accessed | tf_op | source)
XLA Modules:
  0.0 1105.4 jit_solution(739384458572072141)
XLA Ops:
  7.2 1.8 copy.131
  9.1 1.8 copy.133
  11.0 77.3 %all_gather.29 = bf16[96,768]{0,1:T(8,128)(2,1)S(1)} all-gather(bf16[96,24]{0,1:T(8,128)(2,1)} %param.18), channel_id=1, replica_groups=mesh['dp'=32,'ctx'=16] {'dp'}, dimensions={1}, use_global_device_ids=true | all-gather | bytes 152064 | tf_op jit(solution)/shard_map/all_gather | solution.py:78
  92.1 2.1 all-gather.7.cloned.1.call-done
  94.3 7.0 copy.132
  101.3 2.0 copy.136
  103.3 64.5 %all-gather.9.cloned.1.call-done = bf16[2,1024,768]{2,0,1:T(2,128)(2,1)} async-done(((bf16[2,64,768]{2,0,1:T(2,128)(2,1)}), bf16[2,1024,768]{2,0,1:T(2,128)(2,1)}) %all-gather.9.cloned.1.call-update) | async-done | bytes 3145744 | tf_op jit(solution)/shard_map/all_gather | solution.py:82
  167.8 7.0 copy.134
  174.8 2.0 copy.137
  176.9 16.0 %while.37 = (s32[]{:T(128)}, f32[2,2,6,64]{3,2,1,0:T(8,128)}, bf16[2,2,64,384]{3,2,0,1:T(8,128)(2,1)}, bf16[2,2,64,384]{3,2,1,0:T(8,128)(2,1)}, bf16[2,2,1024,38...) while((s32[]{:T(128)}, f32[2,2,6,64]{3,2,1,0:T(8,128)}, ...), condition=%wide.region_3.4_spmd.clone, body=%wide.region_0.3_spmd.clone.sunk | while | flops 209978624 | bytes 21468332 | solution.py:103
  177.6 2.2 constant_dynamic-slice_fusion.23
  185.6 2.2 constant_dynamic-slice_fusion.23
  193.8 43.9 %all-gather.11.cloned.1.call-done = bf16[1536,768]{1,0:T(8,128)(2,1)} async-done(((bf16[96,768]{1,0:T(8,128)(2,1)}), bf16[1536,768]{1,0:T(8,128)(2,1)}) %all-gather.11.cloned.1.call-update) | async-done | bytes 2359312 | tf_op jit(solution)/shard_map/all_gather | solution.py:79
  237.7 2.6 broadcast_select_fusion
  240.3 2.2 collective-permute-start.1
  242.5 7.3 collective-permute-start
  249.8 64.3 %all-gather = bf16[32,48,31]{1,2,0:T(8,128)(2,1)S(1)} all-gather(bf16[1,48,31]{1,2,0:T(8,128)(2,1)S(1)} %bitcast.212), channel_id=1, replica_groups=mesh['dp'=32,'ctx'=16] {'dp'}, dimensions={0}, use_global_device_ids=true | all-gather | bytes 98208 | tf_op jit(solution)/shard_map/all_gather | solution.py:77
  314.8 2.7 fusion.54
  317.5 1.1 fusion.47
  318.6 11.0 collective-permute-start.3
  329.6 6.8 collective-permute-start.2
  336.8 1.3 collective-permute-done.2
  338.3 2.3 fusion.52
  340.9 2.2 bitcast_convert_fusion
  344.2 1.9 fusion.49
  346.1 1.9 fusion.43
  349.2 90.0 %reduce-scatter.6.cloned.1.call-done = bf16[96,768]{1,0:T(8,128)(2,1)} async-done(((bf16[1536,768]{1,0:T(8,128)(2,1)}), bf16[96,768]{1,0:T(8,128)(2,1)}) %reduce-scatter.6.cloned.1.call-update) | async-done | bytes 147472 | tf_op jit(solution)/shard_map/reduce_scatter | solution.py:244
  439.5 1.2 fusion.44
  442.2 1.3 dynamic-slice
  446.6 42.3 %all_gather.33 = f32[2,1024,12]{2,0,1:T(2,128)S(1)} all-gather(f32[2,64,12]{2,0,1:T(2,128)S(1)} %copy.161), channel_id=1, replica_groups=mesh['dp'=32,'ctx'=16] {'ctx'}, dimensions={1}, use_global_device_ids=true | all-gather | bytes 104448 | tf_op jit(solution)/shard_map/all_gather | solution.py:176
  488.9 1.1 copy.162
  490.0 29.2 %all-gather.13.cloned.1.call-done = bf16[2,1024,768]{2,0,1:T(2,128)(2,1)} async-done(((bf16[2,64,768]{2,0,1:T(2,128)(2,1)}), bf16[2,1024,768]{2,0,1:T(2,128)(2,1)}) %all-gather.13.cloned.1.call-update) | async-done | bytes 3145744 | tf_op jit(solution)/shard_map/all_gather | solution.py:184
  519.1 8.7 copy.159
  531.5 29.7 %while.38 = (s32[]{:T(128)}, f32[2,2,64,384]{2,3,1,0:T(8,128)}, bf16[2,2,1024,384]{2,3,1,0:T(8,128)(2,1)}, bf16[2,2,64,384]{3,2,1,0:T(8,128)(2,1)}, f32[2,2,6,64...) while((s32[]{:T(128)}, f32[2,2,64,384]{2,3,1,0:T(8,128)}, ...), condition=%wide.region_6.7_spmd.clone, body=%wide.region_5.6_spmd.clone.sunk | while | flops 306710528 | bytes 19099784 | solution.py:162
  531.5 2.2 constant_dynamic-slice_fusion.25
  533.7 1.6 constant_dynamic-slice_fusion.26
  536.4 2.2 fusion.108
  540.0 1.3 iota_compare_fusion.5
  542.2 3.4 fusion.109
  546.3 2.2 constant_dynamic-slice_fusion.25
  548.5 1.6 constant_dynamic-slice_fusion.26
  550.1 1.1 reshape.235
  551.2 2.2 fusion.108
  554.8 1.3 iota_compare_fusion.5
  557.0 3.4 fusion.109
  561.2 1.2 fusion.56
  563.4 37.6 %all_gather.35 = f32[2,1024,12]{2,0,1:T(2,128)S(1)} all-gather(f32[2,64,12]{2,0,1:T(2,128)} %copy.164), channel_id=1, replica_groups=mesh['dp'=32,'ctx'=16] {'ctx'}, dimensions={1}, use_global_device_ids=true | all-gather | bytes 104448 | tf_op jit(solution)/shard_map/all_gather | solution.py:177
  601.5 59.2 %reduce-scatter.8.cloned.1.call-done = bf16[48,31]{1,0:T(8,128)(2,1)} async-done(((bf16[1536,31]{1,0:T(8,128)(2,1)}), bf16[48,31]{1,0:T(8,128)(2,1)}) %reduce-scatter.8.cloned.1.call-update) | async-done | bytes 2992
  661.6 68.0 %psum.8 = bf16[31,48]{1,0:T(8,128)(2,1)S(1)} all-reduce(bf16[31,48]{1,0:T(8,128)(2,1)S(1)} %copy.181), channel_id=1, replica_groups=mesh['dp'=32,'ctx'=16] {'ctx'}, use_global_device_ids=true, to_apply=%region_11.12 | all-reduce | flops 1488 | bytes 5952 | tf_op jit(solution)/shard_map/psum | solution.py:130
  730.2 222.8 %all-reduce.3.cloned.1.call-done = bf16[96,768]{1,0:T(8,128)(2,1)} async-done(((bf16[96,768]{1,0:T(8,128)(2,1)}), bf16[96,768]{1,0:T(8,128)(2,1)}) %all-reduce.3.cloned.1.call-update) | async-done | bytes 147472
  954.5 91.6 %all-gather.15.cloned.1.call-done = bf16[2,1024,768]{2,1,0:T(8,128)(2,1)} async-done(((bf16[2,64,768]{2,1,0:T(8,128)(2,1)}), bf16[2,1024,768]{2,1,0:T(8,128)(2,1)}) %all-gather.15.cloned.1.call-update) | async-done | bytes 3145744 | tf_op jit(solution)/shard_map/all_gather | solution.py:185
  1046.1 5.8 reshape.203
  1051.9 6.9 copy.163
  1059.8 34.6 %while.39 = (s32[]{:T(128)}, f32[2,2,64,384]{2,3,1,0:T(8,128)}, bf16[2,2,64,384]{2,3,1,0:T(8,128)(2,1)}, bf16[2,2,1024,384]{2,3,0,1:T(8,128)(2,1)}, bf16[2,2,64,...) while((s32[]{:T(128)}, f32[2,2,64,384]{2,3,1,0:T(8,128)}, ...), condition=%wide.region_8.9_spmd.clone, body=%wide.region_7.8_spmd.clone.sunk | while | flops 410517632 | bytes 39764904 | solution.py:224
  1059.8 1.6 constant_dynamic-slice_fusion.28
  1062.5 2.3 fusion.117
  1069.1 3.3 fusion.118
  1073.2 3.0 fusion.119
  1077.1 1.6 constant_dynamic-slice_fusion.28
  1079.8 2.3 fusion.117
  1086.4 3.3 fusion.118
  1090.5 3.0 fusion.119
  1094.4 1.2 fusion.57
  1096.6 1.2 copy.172
  (164 shorter events, 56.3 us)
Async XLA Ops:
  7.2 87.1 %all-gather.7.cloned.1.call-start = ((), (), s32[]{:S(2)}) async-start(), calls=%async_computation.2 | async-start | bytes 3342336 | tf_op jit(solution)/shard_map/all_gather | solution.py:81
  9.0 158.8 %all-gather.9.cloned.1.call-start = ((), (), s32[]{:S(2)}) async-start(), calls=%async_computation.3 | async-start | bytes 3342336 | tf_op jit(solution)/shard_map/all_gather | solution.py:82
  10.9 226.8 %all-gather.11.cloned.1.call-start = ((), (), s32[]{:S(2)}) async-start(), calls=%async_computation.4 | async-start | bytes 2506752 | tf_op jit(solution)/shard_map/all_gather | solution.py:79
  89.1 350.1 %reduce-scatter.6.cloned.1.call-start = ((), (), s32[]{:S(2)}) async-start(), calls=%async_computation.7 | async-start | bytes 2506752 | tf_op jit(solution)/shard_map/reduce_scatter | solution.py:244
  90.8 0.6 copy-start.16
  182.9 1.2 copy-start.12
  184.2 0.7 copy-start.13
  190.9 1.2 copy-start.12
  192.2 0.7 copy-start.13
  192.9 57.0 %copy-start.15 = (bf16[31,48]{1,0:T(8,128)(2,1)S(1)}, bf16[31,48]{1,0:T(8,128)(2,1)}, u32[]{:S(2)}) copy-start(bf16[31,48]{1,0:T(8,128)(2,1)} %param.19) | copy-start | bytes 8932
  240.3 74.3 %collective-permute-start.1 = (bf16[2,15,1536]{2,1,0:T(8,128)(2,1)S(1)}, bf16[2,15,1536]{2,1,0:T(8,128)(2,1)S(1)}, u32[]{:S(2)}, u32[]{:S(2)}) collective-permute-start(bf16[2,15,1536]{2,1,0:T(8,128)(2,1)S(1)} %get-tuple-element.409), channel_id=1, source_target_pairs={{1,0},{2,1},{3,2},{4,3},{5,4},{6,5},{7,6},{8,7},{9,8},{10,9},{11,1... | collective-permute-start | bytes 276488 | tf_op jit(solution)/shard_map/ppermute | solution.py:18
  242.5 72.1 %collective-permute-start = (bf16[2,15,1536]{2,1,0:T(8,128)(2,1)S(1)}, bf16[2,15,1536]{2,1,0:T(8,128)(2,1)S(1)}, u32[]{:S(2)}, u32[]{:S(2)}) collective-permute-start(bf16[2,15,1536]{2,1,0:T(8,128)(2,1)S(1)} %get-tuple-element.408), channel_id=1, source_target_pairs={{0,1},{1,2},{2,3},{3,4},{4,5},{5,6},{6,7},{7,8},{8,9},{9,10},{10,1... | collective-permute-start | bytes 276488 | tf_op jit(solution)/shard_map/ppermute | solution.py:17
  314.8 2.7 copy-start.4
  318.6 18.2 %collective-permute-start.3 = (bf16[2,15,1536]{2,1,0:T(8,128)(2,1)S(1)}, bf16[2,15,1536]{2,1,0:T(8,128)(2,1)S(1)}, u32[]{:S(2)}, u32[]{:S(2)}) collective-permute-start(bf16[2,15,1536]{2,1,0:T(8,128)(2,1)S(1)} %get-tuple-element.407), channel_id=1, source_target_pairs={{1,0},{2,1},{3,2},{4,3},{5,4},{6,5},{7,6},{8,7},{9,8},{10,9},{11,1... | collective-permute-start | bytes 276488 | tf_op jit(solution)/shard_map/ppermute | solution.py:18
  329.6 8.5 collective-permute-start.2
  340.6 2.6 copy-start.9
  340.9 98.6 %copy-start.2 = (bf16[2,64,1536]{2,1,0:T(8,128)(2,1)}, bf16[2,64,1536]{2,1,0:T(8,128)(2,1)S(1)}, u32[]{:S(2)}) copy-start(bf16[2,64,1536]{2,1,0:T(8,128)(2,1)S(1)} %fusion.48) | copy-start | bytes 1179652
  343.1 176.0 %all-gather.13.cloned.1.call-start = ((), (), s32[]{:S(2)}) async-start(), calls=%async_computation.5 | async-start | bytes 3342336 | tf_op jit(solution)/shard_map/all_gather | solution.py:184
  344.1 316.7 %reduce-scatter.8.cloned.1.call-start = ((), (), s32[]{:S(2)}) async-start(), calls=%async_computation.8 | async-start | bytes 405504
  346.1 93.4 %copy-start.1 = (bf16[1536,768]{1,0:T(8,128)(2,1)S(1)}, bf16[1536,768]{1,0:T(8,128)(2,1)}, u32[]{:S(2)}) copy-start(bf16[1536,768]{1,0:T(8,128)(2,1)} %all-gather.11.cloned.1.call-done) | copy-start | bytes 7077892
  348.1 92.6 %copy-start.10 = (bf16[2,64,768]{2,1,0:T(8,128)(2,1)S(1)}, bf16[2,64,768]{2,1,0:T(8,128)(2,1)}, u32[]{:S(2)}) copy-start(bf16[2,64,768]{2,1,0:T(8,128)(2,1)} %param.16) | copy-start | bytes 589828
  348.1 92.6 %copy-start.11 = (bf16[2,64,768]{2,1,0:T(8,128)(2,1)S(1)}, bf16[2,64,768]{2,1,0:T(8,128)(2,1)}, u32[]{:S(2)}) copy-start(bf16[2,64,768]{2,1,0:T(8,128)(2,1)} %param.17) | copy-start | bytes 589828
  348.1 96.8 %copy-start.14 = (bf16[2,2,64,384]{3,2,0,1:T(8,128)(2,1)S(1)}, bf16[2,2,64,384]{3,2,0,1:T(8,128)(2,1)}, u32[]{:S(2)}) copy-start(bf16[2,2,64,384]{3,2,0,1:T(8,128)(2,1)} %get-tuple-element.145) | copy-start | bytes 589828
  349.1 603.8 %all-reduce.3.cloned.1.call-start = ((), (), s32[]{:S(2)}) async-start(), calls=%async_computation.9 | async-start | bytes 294912
  439.2 606.9 %all-gather.15.cloned.1.call-start = ((), (), s32[]{:S(2)}) async-start(), calls=%async_computation.6 | async-start | bytes 3342336 | tf_op jit(solution)/shard_map/all_gather | solution.py:185
  490.0 37.9 %copy-start.3 = (bf16[2,64,768]{2,1,0:T(8,128)(2,1)S(1)}, bf16[2,64,768]{2,1,0:T(8,128)(2,1)}, u32[]{:S(2)}) copy-start(bf16[2,64,768]{2,1,0:T(8,128)(2,1)} %fusion.44) | copy-start | bytes 589828
  1051.9 7.8 copy-start.17
  1059.8 5.6 copy-start.7
  1062.5 2.8 copy-start
  1073.2 3.0 copy-start.5
  1073.2 3.8 copy-start.8
  1076.3 0.7 copy-start.6
  1077.1 5.6 copy-start.7
  1079.8 2.8 copy-start
  1090.5 3.0 copy-start.5
  1090.5 3.8 copy-start.8
  1093.6 0.7 copy-start.6
Sparse Core Ops, SparseCore 0:
  11.8 82.3 all-gather.6
  98.1 69.6 all-gather.8
  171.7 65.9 all-gather.10
  343.3 95.8 reduce-scatter.5
  442.9 76.1 all-gather.12
  521.8 138.9 reduce-scatter.7
  663.9 288.9 all-reduce.2
  956.3 89.7 all-gather.14
where the time goes:
time: 1110 us
  waiting for transfers between devices  605 us (55%)
  blocking collectives  290 us (26%)
  local copies, waits for them, and re-layouts  105 us (9%)
  matrix products  46.7 us (4%)
  starting transfers between devices  27.7 us (2%)
  other arithmetic  15.8 us (1%)
  between operations  15.2 us (1%)
    unnamed x10, waiting for transfers between devices  282 us
    all_gather x1, waiting for transfers between devices, per_device(): lax.all_gather(grad_attended, 'ctx', axis=1, tiled=True)  91.6 us
    reduce_scatter x1, waiting for transfers between devices, per_device(): lax.psum_scatter(jnp.einsum('ufd,ufe->de', hidden_cols, attended, preferr...  90 us
    all_gather x1, blocking collectives, per_device(): panel_rows = lax.all_gather(out_weight, 'dp', axis=1, tiled=True)  77.3 us
    psum x1, blocking collectives, per_device(): kernel_whole = lax.psum(kernel_term.astype(jnp.bfloat16), 'ctx')  68 us
    all_gather x1, waiting for transfers between devices, per_device(): lax.all_gather(value_proj, 'ctx', axis=1, tiled=True)  64.5 us
    all_gather x1, blocking collectives, per_device(): lax.all_gather(conv_weight, 'dp', axis=1, tiled=True).astype(jnp.float32)  64.3 us
    all_gather x1, waiting for transfers between devices, per_device(): weight_full = lax.all_gather(panel_rows, 'ctx', axis=0, tiled=True)  43.9 us
  transfers between devices with their start and end apart: 12, of which 9 were waited for; matrix products, arithmetic and copies ran while one was open for 9% of the time, Pallas kernels for 0%

commit v1 on v0

--- a/solution.py
+++ b/solution.py
@@ -127,7 +127,7 @@
             kernel_term
             + depthwise(padded[utt_index : utt_index + 1], grad_conv_wide[utt_index][:, None, :])[0]
         )
-    kernel_whole = lax.psum(kernel_term.astype(jnp.bfloat16), "ctx")
+    kernel_whole = jnp.sum(lax.all_gather(kernel_term.astype(jnp.bfloat16), "ctx"), axis=0)
     grad_conv_weight = lax.psum_scatter(kernel_whole, "dp", scatter_dimension=1, tiled=True).astype(
         jnp.float32
     )

time: 1110 us -> 1160 us (1.045)
  waiting for transfers between devices: 605 us -> 719 us
  blocking collectives: 290 us -> 224 us
    psum x1 -> x0, blocking collectives: 68 us -> none  [per_device(): kernel_whole = lax.psum(kernel_term.astype(jnp.bfloat16), 'ctx')]
    unnamed x10 -> x11, waiting for transfers between devices: 282 us -> 346 us
    all_gather x0 -> x1, waiting for transfers between devices: none -> 45.4 us  [per_device(): lax.all_gather(kernel_term.astype(jnp.bfloat16), 'ctx')]
  transfers between devices with their start and end apart: 12 -> 13, of which waited for: 9 -> 10; matrix products, arithmetic and copies ran while one was open for 9% -> 9% of each run, Pallas kernels for 0% -> 0%
where the time goes in v1:
time: 1160 us
  waiting for transfers between devices  719 us (62%)
  blocking collectives  224 us (19%)
  local copies, waits for them, and re-layouts  106 us (9%)
  matrix products  46.6 us (4%)
  starting transfers between devices  27.8 us (2%)
  other arithmetic  17.5 us (2%)
  between operations  14.9 us (1%)
    unnamed x11, waiting for transfers between devices  346 us
    reduce_scatter x1, waiting for transfers between devices, per_device(): lax.psum_scatter(jnp.einsum('ufd,ufe->de', hidden_cols, attended, preferr...  95 us
    all_gather x1, waiting for transfers between devices, per_device(): lax.all_gather(grad_attended, 'ctx', axis=1, tiled=True)  91.6 us
    all_gather x1, blocking collectives, per_device(): panel_rows = lax.all_gather(out_weight, 'dp', axis=1, tiled=True)  77.3 us
    all_gather x1, waiting for transfers between devices, per_device(): lax.all_gather(value_proj, 'ctx', axis=1, tiled=True)  64.6 us
    all_gather x1, blocking collectives, per_device(): lax.all_gather(conv_weight, 'dp', axis=1, tiled=True).astype(jnp.float32)  64.3 us
    all_gather x1, waiting for transfers between devices, per_device(): lax.all_gather(kernel_term.astype(jnp.bfloat16), 'ctx')  45.4 us
    all_gather x1, waiting for transfers between devices, per_device(): weight_full = lax.all_gather(panel_rows, 'ctx', axis=0, tiled=True)  43.9 us
  transfers between devices with their start and end apart: 13, of which 10 were waited for; matrix products, arithmetic and copies ran while one was open for 9% of the time, Pallas kernels for 0%

profile of v1, /device:TPU:1, one launch (start us, length us, event | category | flops | bytes accessed | tf_op | source)
XLA Modules:
  0.0 1156.0 jit_solution(6337697547938895316)
XLA Ops:
  7.2 1.8 copy.132
  9.1 1.8 copy.134
  11.0 77.3 %all_gather.33 = bf16[96,768]{0,1:T(8,128)(2,1)S(1)} all-gather(bf16[96,24]{0,1:T(8,128)(2,1)} %param.18), channel_id=1, replica_groups=mesh['dp'=32,'ctx'=16] {'dp'}, dimensions={1}, use_global_device_ids=true | all-gather | bytes 152064 | tf_op jit(solution)/shard_map/all_gather | solution.py:78
  92.1 2.2 all-gather.8.cloned.1.call-done
  94.3 7.0 copy.133
  101.3 2.0 copy.137
  103.3 64.6 %all-gather.10.cloned.1.call-done = bf16[2,1024,768]{2,0,1:T(2,128)(2,1)} async-done(((bf16[2,64,768]{2,0,1:T(2,128)(2,1)}), bf16[2,1024,768]{2,0,1:T(2,128)(2,1)}) %all-gather.10.cloned.1.call-update) | async-done | bytes 3145744 | tf_op jit(solution)/shard_map/all_gather | solution.py:82
  167.8 7.0 copy.135
  174.8 2.0 copy.138
  176.8 16.0 %while.37 = (s32[]{:T(128)}, f32[2,2,6,64]{3,2,1,0:T(8,128)}, bf16[2,2,64,384]{3,2,0,1:T(8,128)(2,1)}, bf16[2,2,64,384]{3,2,1,0:T(8,128)(2,1)}, bf16[2,2,1024,38...) while((s32[]{:T(128)}, f32[2,2,6,64]{3,2,1,0:T(8,128)}, ...), condition=%wide.region_3.4_spmd.clone, body=%wide.region_0.3_spmd.clone.sunk | while | flops 209978624 | bytes 21468332 | solution.py:103
  177.6 2.2 constant_dynamic-slice_fusion.23
  185.6 2.2 constant_dynamic-slice_fusion.23
  193.8 43.9 %all-gather.12.cloned.1.call-done = bf16[1536,768]{1,0:T(8,128)(2,1)} async-done(((bf16[96,768]{1,0:T(8,128)(2,1)}), bf16[1536,768]{1,0:T(8,128)(2,1)}) %all-gather.12.cloned.1.call-update) | async-done | bytes 2359312 | tf_op jit(solution)/shard_map/all_gather | solution.py:79
  237.7 2.6 broadcast_select_fusion
  240.3 2.2 collective-permute-start.1
  242.5 7.3 collective-permute-start
  249.8 64.3 %all-gather = bf16[32,48,31]{1,2,0:T(8,128)(2,1)S(1)} all-gather(bf16[1,48,31]{1,2,0:T(8,128)(2,1)S(1)} %bitcast.210), channel_id=1, replica_groups=mesh['dp'=32,'ctx'=16] {'dp'}, dimensions={0}, use_global_device_ids=true | all-gather | bytes 98208 | tf_op jit(solution)/shard_map/all_gather | solution.py:77
  314.8 2.7 fusion.54
  317.5 1.1 fusion.47
  318.7 1.9 fusion.49
  320.5 1.9 fusion.43
  323.2 11.0 collective-permute-start.3
  334.2 6.8 collective-permute-start.2
  341.4 1.3 collective-permute-done.2
  342.9 2.3 fusion.52
  345.5 2.2 bitcast_convert_fusion
  348.8 45.4 %all-gather.18.cloned.1.call-done = bf16[16,31,1536]{2,1,0:T(8,128)(2,1)} async-done(((bf16[1,31,1536]{2,1,0:T(8,128)(2,1)}), bf16[16,31,1536]{2,1,0:T(8,128)(2,1)}) %all-gather.18.cloned.1.call-update) | async-done | bytes 1523728 | tf_op jit(solution)/shard_map/all_gather | solution.py:130
  394.2 1.7 reduce_sum.31
  397.0 95.0 %reduce-scatter.6.cloned.1.call-done = bf16[96,768]{1,0:T(8,128)(2,1)} async-done(((bf16[1536,768]{1,0:T(8,128)(2,1)}), bf16[96,768]{1,0:T(8,128)(2,1)}) %reduce-scatter.6.cloned.1.call-update) | async-done | bytes 147472 | tf_op jit(solution)/shard_map/reduce_scatter | solution.py:244
  492.3 1.2 fusion.44
  495.0 1.3 dynamic-slice
  499.3 42.4 %all_gather.37 = f32[2,1024,12]{2,0,1:T(2,128)S(1)} all-gather(f32[2,64,12]{2,0,1:T(2,128)S(1)} %copy.162), channel_id=1, replica_groups=mesh['dp'=32,'ctx'=16] {'ctx'}, dimensions={1}, use_global_device_ids=true | all-gather | bytes 104448 | tf_op jit(solution)/shard_map/all_gather | solution.py:176
  541.7 1.1 copy.163
  542.8 28.9 %all-gather.14.cloned.1.call-done = bf16[2,1024,768]{2,0,1:T(2,128)(2,1)} async-done(((bf16[2,64,768]{2,0,1:T(2,128)(2,1)}), bf16[2,1024,768]{2,0,1:T(2,128)(2,1)}) %all-gather.14.cloned.1.call-update) | async-done | bytes 3145744 | tf_op jit(solution)/shard_map/all_gather | solution.py:184
  571.7 8.7 copy.160
  584.0 29.7 %while.38 = (s32[]{:T(128)}, f32[2,2,64,384]{2,3,1,0:T(8,128)}, bf16[2,2,1024,384]{2,3,1,0:T(8,128)(2,1)}, bf16[2,2,64,384]{3,2,1,0:T(8,128)(2,1)}, f32[2,2,6,64...) while((s32[]{:T(128)}, f32[2,2,64,384]{2,3,1,0:T(8,128)}, ...), condition=%wide.region_6.7_spmd.clone, body=%wide.region_5.6_spmd.clone.sunk | while | flops 306710528 | bytes 19099784 | solution.py:162
  584.0 2.2 constant_dynamic-slice_fusion.25
  586.2 1.6 constant_dynamic-slice_fusion.26
  588.9 2.2 fusion.108
  592.5 1.3 iota_compare_fusion.5
  594.7 3.4 fusion.109
  598.9 2.2 constant_dynamic-slice_fusion.25
  601.1 1.6 constant_dynamic-slice_fusion.26
  603.8 2.2 fusion.108
  607.4 1.3 iota_compare_fusion.5
  609.6 3.4 fusion.109
  613.8 1.2 fusion.56
  616.0 39.9 %all_gather.39 = f32[2,1024,12]{2,0,1:T(2,128)S(1)} all-gather(f32[2,64,12]{2,0,1:T(2,128)} %copy.165), channel_id=1, replica_groups=mesh['dp'=32,'ctx'=16] {'ctx'}, dimensions={1}, use_global_device_ids=true | all-gather | bytes 104448 | tf_op jit(solution)/shard_map/all_gather | solution.py:177
  656.3 57.5 %reduce-scatter.8.cloned.1.call-done = bf16[48,31]{1,0:T(8,128)(2,1)} async-done(((bf16[1536,31]{1,0:T(8,128)(2,1)}), bf16[48,31]{1,0:T(8,128)(2,1)}) %reduce-scatter.8.cloned.1.call-update) | async-done | bytes 2992
  715.2 288.5 %all-reduce.3.cloned.1.call-done = bf16[96,768]{1,0:T(8,128)(2,1)} async-done(((bf16[96,768]{1,0:T(8,128)(2,1)}), bf16[96,768]{1,0:T(8,128)(2,1)}) %all-reduce.3.cloned.1.call-update) | async-done | bytes 147472
  1005.3 91.6 %all-gather.16.cloned.1.call-done = bf16[2,1024,768]{2,1,0:T(8,128)(2,1)} async-done(((bf16[2,64,768]{2,1,0:T(8,128)(2,1)}), bf16[2,1024,768]{2,1,0:T(8,128)(2,1)}) %all-gather.16.cloned.1.call-update) | async-done | bytes 3145744 | tf_op jit(solution)/shard_map/all_gather | solution.py:185
  1097.0 5.8 reshape.201
  1102.8 6.8 copy.164
  1110.6 34.6 %while.39 = (s32[]{:T(128)}, f32[2,2,64,384]{2,3,1,0:T(8,128)}, bf16[2,2,64,384]{2,3,1,0:T(8,128)(2,1)}, bf16[2,2,1024,384]{2,3,0,1:T(8,128)(2,1)}, bf16[2,2,64,...) while((s32[]{:T(128)}, f32[2,2,64,384]{2,3,1,0:T(8,128)}, ...), condition=%wide.region_8.9_spmd.clone, body=%wide.region_7.8_spmd.clone.sunk | while | flops 410517632 | bytes 39764904 | solution.py:224
  1110.6 1.6 constant_dynamic-slice_fusion.28
  1113.3 2.2 fusion.117
  1119.9 3.3 fusion.118
  1124.0 3.0 fusion.119
  1127.9 1.6 constant_dynamic-slice_fusion.28
  1130.6 2.3 fusion.117
  1137.2 3.3 fusion.118
  1141.4 3.0 fusion.119
  1145.2 1.2 fusion.57
  1147.4 1.2 copy.173
  (168 shorter events, 58.0 us)
Async XLA Ops:
  7.2 87.1 %all-gather.8.cloned.1.call-start = ((), (), s32[]{:S(2)}) async-start(), calls=%async_computation.2 | async-start | bytes 3342336 | tf_op jit(solution)/shard_map/all_gather | solution.py:81
  9.0 158.8 %all-gather.10.cloned.1.call-start = ((), (), s32[]{:S(2)}) async-start(), calls=%async_computation.3 | async-start | bytes 3342336 | tf_op jit(solution)/shard_map/all_gather | solution.py:82
  10.9 226.8 %all-gather.12.cloned.1.call-start = ((), (), s32[]{:S(2)}) async-start(), calls=%async_computation.4 | async-start | bytes 2506752 | tf_op jit(solution)/shard_map/all_gather | solution.py:79
  89.1 305.1 %all-gather.18.cloned.1.call-start = ((), (), s32[]{:S(2)}) async-start(), calls=%async_computation.8 | async-start | bytes 1671168 | tf_op jit(solution)/shard_map/all_gather | solution.py:130
  90.8 0.5 copy-start.16
  182.9 1.2 copy-start.12
  184.2 0.7 copy-start.13
  190.9 1.2 copy-start.12
  192.2 0.7 copy-start.13
  192.8 57.0 %copy-start.15 = (bf16[31,48]{1,0:T(8,128)(2,1)S(1)}, bf16[31,48]{1,0:T(8,128)(2,1)}, u32[]{:S(2)}) copy-start(bf16[31,48]{1,0:T(8,128)(2,1)} %param.19) | copy-start | bytes 8932
  240.3 74.3 %collective-permute-start.1 = (bf16[2,15,1536]{2,1,0:T(8,128)(2,1)S(1)}, bf16[2,15,1536]{2,1,0:T(8,128)(2,1)S(1)}, u32[]{:S(2)}, u32[]{:S(2)}) collective-permute-start(bf16[2,15,1536]{2,1,0:T(8,128)(2,1)S(1)} %get-tuple-element.409), channel_id=1, source_target_pairs={{1,0},{2,1},{3,2},{4,3},{5,4},{6,5},{7,6},{8,7},{9,8},{10,9},{11,1... | collective-permute-start | bytes 276488 | tf_op jit(solution)/shard_map/ppermute | solution.py:18
  242.5 72.1 %collective-permute-start = (bf16[2,15,1536]{2,1,0:T(8,128)(2,1)S(1)}, bf16[2,15,1536]{2,1,0:T(8,128)(2,1)S(1)}, u32[]{:S(2)}, u32[]{:S(2)}) collective-permute-start(bf16[2,15,1536]{2,1,0:T(8,128)(2,1)S(1)} %get-tuple-element.408), channel_id=1, source_target_pairs={{0,1},{1,2},{2,3},{3,4},{4,5},{5,6},{6,7},{7,8},{8,9},{9,10},{10,1... | collective-permute-start | bytes 276488 | tf_op jit(solution)/shard_map/ppermute | solution.py:17
  314.8 2.7 copy-start.4
  323.2 168.8 %reduce-scatter.6.cloned.1.call-start = ((), (), s32[]{:S(2)}) async-start(), calls=%async_computation.7 | async-start | bytes 2506752 | tf_op jit(solution)/shard_map/reduce_scatter | solution.py:244
  323.2 18.2 %collective-permute-start.3 = (bf16[2,15,1536]{2,1,0:T(8,128)(2,1)S(1)}, bf16[2,15,1536]{2,1,0:T(8,128)(2,1)S(1)}, u32[]{:S(2)}, u32[]{:S(2)}) collective-permute-start(bf16[2,15,1536]{2,1,0:T(8,128)(2,1)S(1)} %get-tuple-element.407), channel_id=1, source_target_pairs={{1,0},{2,1},{3,2},{4,3},{5,4},{6,5},{7,6},{8,7},{9,8},{10,9},{11,1... | collective-permute-start | bytes 276488 | tf_op jit(solution)/shard_map/ppermute | solution.py:18
  334.2 8.5 collective-permute-start.2
  345.2 2.6 copy-start.9
  345.5 146.7 %copy-start.2 = (bf16[2,64,1536]{2,1,0:T(8,128)(2,1)}, bf16[2,64,1536]{2,1,0:T(8,128)(2,1)S(1)}, u32[]{:S(2)}) copy-start(bf16[2,64,1536]{2,1,0:T(8,128)(2,1)S(1)} %fusion.48) | copy-start | bytes 1179652
  347.8 144.5 %copy-start.1 = (bf16[1536,768]{1,0:T(8,128)(2,1)S(1)}, bf16[1536,768]{1,0:T(8,128)(2,1)}, u32[]{:S(2)}) copy-start(bf16[1536,768]{1,0:T(8,128)(2,1)} %all-gather.12.cloned.1.call-done) | copy-start | bytes 7077892
  347.8 145.7 %copy-start.10 = (bf16[2,64,768]{2,1,0:T(8,128)(2,1)S(1)}, bf16[2,64,768]{2,1,0:T(8,128)(2,1)}, u32[]{:S(2)}) copy-start(bf16[2,64,768]{2,1,0:T(8,128)(2,1)} %param.16) | copy-start | bytes 589828
  347.8 223.9 %all-gather.14.cloned.1.call-start = ((), (), s32[]{:S(2)}) async-start(), calls=%async_computation.5 | async-start | bytes 3342336 | tf_op jit(solution)/shard_map/all_gather | solution.py:184
  348.8 144.7 %copy-start.11 = (bf16[2,64,768]{2,1,0:T(8,128)(2,1)S(1)}, bf16[2,64,768]{2,1,0:T(8,128)(2,1)}, u32[]{:S(2)}) copy-start(bf16[2,64,768]{2,1,0:T(8,128)(2,1)} %param.17) | copy-start | bytes 589828
  348.8 365.1 %reduce-scatter.8.cloned.1.call-start = ((), (), s32[]{:S(2)}) async-start(), calls=%async_computation.9 | async-start | bytes 405504
  395.9 101.7 %copy-start.14 = (bf16[2,2,64,384]{3,2,0,1:T(8,128)(2,1)S(1)}, bf16[2,2,64,384]{3,2,0,1:T(8,128)(2,1)}, u32[]{:S(2)}) copy-start(bf16[2,2,64,384]{3,2,0,1:T(8,128)(2,1)} %get-tuple-element.145) | copy-start | bytes 589828
  396.9 606.9 %all-reduce.3.cloned.1.call-start = ((), (), s32[]{:S(2)}) async-start(), calls=%async_computation.10 | async-start | bytes 294912
  492.0 604.9 %all-gather.16.cloned.1.call-start = ((), (), s32[]{:S(2)}) async-start(), calls=%async_computation.6 | async-start | bytes 3342336 | tf_op jit(solution)/shard_map/all_gather | solution.py:185
  542.8 37.6 %copy-start.3 = (bf16[2,64,768]{2,1,0:T(8,128)(2,1)S(1)}, bf16[2,64,768]{2,1,0:T(8,128)(2,1)}, u32[]{:S(2)}) copy-start(bf16[2,64,768]{2,1,0:T(8,128)(2,1)} %fusion.44) | copy-start | bytes 589828
  1102.8 7.8 copy-start.17
  1110.6 5.6 copy-start.7
  1113.3 2.8 copy-start
  1124.0 3.0 copy-start.5
  1124.0 3.8 copy-start.8
  1127.1 0.8 copy-start.6
  1127.9 5.6 copy-start.7
  1130.6 2.8 copy-start
  1141.4 3.0 copy-start.5
  1141.4 3.8 copy-start.8
  1144.4 0.8 copy-start.6
Sparse Core Ops, SparseCore 0:
  11.8 82.3 all-gather.7
  98.1 69.6 all-gather.9
  171.7 65.9 all-gather.11
  323.3 70.9 all-gather.17
  398.9 93.0 reduce-scatter.5
  495.7 76.0 all-gather.13
  574.5 139.2 reduce-scatter.7
  717.0 286.7 all-reduce.2
  1007.1 89.7 all-gather.15
